TPU v7x, 32 devices: a whole 2x2x4 slice. The times are simulated.
32 devices in a mesh: section: 2 (over y), hid: 4 (over z), wid: 4 (over x, core).
Axes of the slice: x: 2, y: 2, z: 4, core: 2. Of those that a mesh axis runs over, the one named last changes fastest.
Arguments:
- weights: bfloat16 [2, 6144, 24576], P('section', 'hid', 'wid'), may hold values from -0.078125 to 0.078125
- preact: bfloat16 [1024, 24576], P(('section', 'hid'), 'wid'), may hold values from -6 to 6
- inputs: bfloat16 [1024, 6144], P(('section', 'wid'), 'hid'), may hold values from -6 to 6
- grad_out: bfloat16 [1024, 6144], P(('section', 'wid'), 'hid'), may hold values from -6 to 6
- row_state: float32 [2, 6144], P('section', 'hid'), may hold values from 32 to 256
- col_state: float32 [2, 24576], P('section', 'wid'), may hold values from 32 to 256
Outputs:
- input_grad: float32 [1024, 6144], P(('section', 'wid'), 'hid')
- update: float32 [2, 6144, 24576], P('section', 'hid', 'wid')
All inputs are finite; a program needn't handle non-finite values.
Results may differ from a plain program's by a relative error of at most 0.0029.
Values may be sent and summed in bfloat16 or wider, within the bound.
A program may use at most 192 MiB of HBM per device.

v0:
```python
import jax
import jax.numpy as jnp
from jax import lax
from jax.sharding import PartitionSpec as P

D = 6144
FF = 24576


decay_rate = 0.9
root_half = 0.7071067811865476
inv_root_tau = 0.3989422804014327


def from_behind(block, axis, distance):
    devices = range(lax.axis_size(axis))
    route = [((i - distance) % len(devices), i) for i in devices]
    return lax.ppermute(block, axis, route)


def normal_cdf(pre):
    return 0.5 * (1.0 + lax.erf(pre * root_half))


def gelu_value(pre):
    return pre * normal_cdf(pre)


def gelu_slope(pre):
    return normal_cdf(pre) + pre * jnp.exp(-0.5 * pre * pre) * inv_root_tau


def contract(left, right):
    return lax.dot_general(
        left, right, (((0,), (0,)), ((), ())), preferred_element_type=jnp.float32
    )


def shards(weights, preact, inputs, grad_out, row_state, col_state):
    own_tile = weights[0]
    first_section = lax.axis_index("section") == 0
    other_tile = from_behind(own_tile, "section", 1)
    up_tile = jnp.where(first_section, own_tile, other_tile)
    down_tile = jnp.where(first_section, other_tile, own_tile)
    grad_half, input_half = (
        lax.all_gather(grad_out, "wid", axis=0, tiled=True),
        lax.all_gather(inputs, "wid", axis=0, tiled=True),
    )
    pre_half = lax.all_gather(preact, "hid", axis=0, tiled=True)
    pre_float = pre_half.astype(jnp.float32)
    activation = gelu_value(pre_float).astype(jnp.bfloat16)
    grad_rows = grad_half
    hidden_share = lax.psum_scatter(
        jnp.dot(grad_rows, down_tile, preferred_element_type=jnp.float32),
        "hid",
        scatter_dimension=0,
        tiled=True,
    )
    pre_share = (hidden_share * gelu_slope(preact.astype(jnp.float32))).astype(jnp.bfloat16)
    pre_grad = lax.all_gather(pre_share, "hid", axis=0, tiled=True)
    grad_rows = pre_grad
    input_sum = lax.psum_scatter(
        lax.dot_general(
            grad_rows, up_tile, (((1,), (1,)), ((), ())), preferred_element_type=jnp.float32
        ),
        "wid",
        scatter_dimension=0,
        tiled=True,
    )
    input_grad = input_sum + grad_out.astype(jnp.float32)
    own_left = jnp.where(first_section, input_half, grad_half)
    own_right = jnp.where(first_section, pre_grad, activation)
    give_left = jnp.where(first_section, grad_half, input_half)
    give_right = jnp.where(first_section, activation, pre_grad)
    gradient = contract(own_left, own_right)
    left_width = give_left.shape[1]
    joined = jnp.concatenate([give_left, give_right], axis=1)
    received = from_behind(joined, "section", 1)
    gradient = gradient + contract(received[:, :left_width], received[:, left_width:])
    squares = gradient * gradient
    row_local = jnp.sum(squares, axis=1)
    col_local = jnp.sum(squares, axis=0)
    row_prev = row_state[0]
    col_prev = col_state[0]
    row_total = lax.psum(row_local, "wid")
    row_moment = decay_rate * row_prev + (1.0 - decay_rate) / FF * row_total
    col_total, row_sum = lax.psum((col_local, jnp.sum(row_moment)), "hid")
    col_moment = decay_rate * col_prev + (1.0 - decay_rate) / D * col_total
    row_mean = row_sum / D
    update = gradient * lax.rsqrt(row_moment[:, None] * col_moment[None, :] / row_mean)
    return (input_grad, update[None])


def solution(mesh):
    placed = (
        P("section", "hid", "wid"),
        P(("section", "hid"), "wid"),
        P(("section", "wid"), "hid"),
        P(("section", "wid"), "hid"),
        P("section", "hid"),
        P("section", "wid"),
    )
    return jax.shard_map(
        shards,
        mesh=mesh,
        in_specs=placed,
        out_specs=(P(("section", "wid"), "hid"), P("section", "hid", "wid")),
        check_vma=False,
    )
```

profile of v0, /device:TPU:0, one launch (start us, length us, event | category | flops | bytes accessed | tf_op | source)
XLA Modules:
  0.0 1178.8 jit_solution(11797534428159010847)
XLA Ops:
  7.2 0.0 all-gather.5.cloned.1.call-start
  7.2 3.0 collective-permute-start
  10.2 1.9 copy.8
  12.2 0.0 all-gather.5.cloned.1.call-update
  12.2 0.0 reduce-scatter.3.cloned.1.call-start
  12.2 20.5 %all-gather.5.cloned.1.call-done = bf16[512,1536]{0,1:T(8,128)(2,1)} async-done(((bf16[128,1536]{0,1:T(8,128)(2,1)}), bf16[512,1536]{0,1:T(8,128)(2,1)}) %all-gather.5.cloned.1.call-update) | async-done | bytes 1572880 | tf_op jit(solution)/shard_map/all_gather | solution.py:46
  32.7 383.0 %collective-permute-done = bf16[1536,6144]{1,0:T(8,128)(2,1)} collective-permute-done((bf16[1536,6144]{1,0:T(8,128)(2,1)}, bf16[1536,6144]{1,0:T(8,128)(2,1)}, u32[]{:S(2)}, u32[]{:S(2)}) %collective-permute-start) | collective-permute-done | bytes 18874400 | tf_op jit(solution)/shard_map/ppermute | solution.py:18
  415.7 20.1 %fusion.10 = f32[512,6144]{0,1:T(8,128)} fusion(bf16[512,1536]{0,1:T(8,128)(2,1)} %all-gather.5.cloned.1.call-done, bf16[1536,6144]{1,0:T(8,128)(2,1)} %collective-permute-done, pred[]{:T(512)S(6)} %eq.3, bf16[1,1536,6144]{2,1,0:T(8,128)(2,1)} %param.6), kind=kOutput, calls=%fused_computation.16 | convolution fusion | flops 9673113600 | bytes 51904512 | tf_op jit(solution)/shard_map/dot_general | solution.py:54
  435.9 0.0 copy-start.5
  435.9 0.0 copy-start.3
  435.9 0.0 reduce-scatter.3.cloned.1.call-update
  435.9 0.0 all-gather.9.cloned.1.call-start
  435.9 0.9 copy-done.5
  436.9 0.9 copy.10
  437.8 0.0 all-gather.9.cloned.1.call-update
  437.8 0.0 copy-start
  437.8 0.0 all-gather.11.cloned.1.call-start
  437.9 0.0 copy-done.3
  437.9 1.6 copy.9
  439.4 0.0 all-gather.11.cloned.1.call-update
  439.5 0.0 all-gather.7.cloned.1.call-start
  439.5 208.9 %reduce-scatter.3.cloned.1.call-done = f32[128,6144]{0,1:T(8,128)} async-done(((f32[512,6144]{0,1:T(8,128)}), f32[128,6144]{0,1:T(8,128)}) %reduce-scatter.3.cloned.1.call-update) | async-done | bytes 3145744 | tf_op jit(solution)/shard_map/reduce_scatter | solution.py:53
  648.4 3.9 fusion.24
  652.4 0.0 all-gather.7.cloned.1.call-update
  652.4 0.2 reduce-scatter.5.cloned.1.call-start
  652.6 18.8 %all-gather.9.cloned.1.call-done = bf16[512,1536]{0,1:T(8,128)(2,1)} async-done(((bf16[128,1536]{0,1:T(8,128)(2,1)}), bf16[512,1536]{0,1:T(8,128)(2,1)}) %all-gather.9.cloned.1.call-update) | async-done | bytes 1572880 | tf_op jit(solution)/shard_map/all_gather | solution.py:47
  671.5 0.0 copy-done
  671.5 1.3 broadcast_select_fusion.1
  672.8 115.0 %all-gather.11.cloned.1.call-done = bf16[512,6144]{0,1:T(8,128)(2,1)} async-done(((bf16[128,6144]{0,1:T(8,128)(2,1)}), bf16[512,6144]{0,1:T(8,128)(2,1)}) %all-gather.11.cloned.1.call-update) | async-done | bytes 6291472 | tf_op jit(solution)/shard_map/all_gather | solution.py:49
  787.8 115.0 %all-gather.7.cloned.1.call-done = bf16[512,6144]{0,1:T(8,128)(2,1)} async-done(((bf16[128,6144]{0,1:T(8,128)(2,1)}), bf16[512,6144]{0,1:T(8,128)(2,1)}) %all-gather.7.cloned.1.call-update) | async-done | bytes 6291472 | tf_op jit(solution)/shard_map/all_gather | solution.py:60
  902.8 6.1 broadcast_select_fusion
  908.9 5.1 pad_maximum_fusion
  914.0 0.0 copy-start.8
  914.0 0.0 copy-start.7
  914.0 0.0 copy-start.1
  914.0 0.0 copy-start.2
  914.0 2.6 collective-permute-start.1
  916.6 16.2 %fusion = f32[512,1536]{1,0:T(8,128)} fusion(bf16[512,6144]{0,1:T(8,128)(2,1)} %all-gather.7.cloned.1.call-done, bf16[1536,6144]{1,0:T(8,128)(2,1)} %collective-permute-done, pred[]{:T(512)S(6)} %eq.3, bf16[1,1536,6144]{2,1,0:T(8,128)(2,1)} %param.6), kind=kOutput, calls=%fused_computation.4 | convolution fusion | flops 9673113600 | bytes 47185920 | tf_op jit(solution)/shard_map/dot_general | solution.py:63
  932.7 0.0 reduce-scatter.5.cloned.1.call-update
  932.8 0.0 copy-done.8
  932.8 0.0 copy-done.7
  932.8 0.6 broadcast_multiply_fusion
  933.5 0.0 copy-done.1
  933.5 0.0 copy-done.2
  933.5 0.0 copy-start.4
  933.5 21.2 %fusion.14 = f32[1536,6144]{1,0:T(8,128)} fusion(bf16[512,6144]{0,1:T(8,128)(2,1)} %all-gather.7.cloned.1.call-done, pred[]{:T(512)S(6)} %eq.3, bf16[512,1536]{0,1:T(8,128)(2,1)S(1)} %copy-done.2, bf16[512,1536]{0,1:T(8,128)(2,1)S(1)} %copy-done.1, bf16[512,6144]{0,1:T(8,128)(2,1)} %all-gather.11.cloned.1.call-done), kind=kOutput, calls=%fused_computation.19 | convolution fusion | flops 9686482944 | bytes 53477376 | tf_op jit(solution)/shard_map/dot_general | solution.py:34
  954.6 16.8 %reduce-scatter.5.cloned.1.call-done = f32[128,1536]{1,0:T(8,128)} async-done(((f32[512,1536]{1,0:T(8,128)}), f32[128,1536]{1,0:T(8,128)}) %reduce-scatter.5.cloned.1.call-update) | async-done | bytes 786448 | tf_op jit(solution)/shard_map/reduce_scatter | solution.py:62
  971.4 0.0 copy-done.4
  971.4 2.1 convert_add_fusion
  973.5 0.0 copy-start.6
  973.5 112.9 %collective-permute-done.1 = bf16[512,7680]{0,1:T(8,128)(2,1)} collective-permute-done((bf16[512,7680]{0,1:T(8,128)(2,1)}, bf16[512,7680]{0,1:T(8,128)(2,1)}, u32[]{:S(2)}, u32[]{:S(2)}) %collective-permute-start.1) | collective-permute-done | bytes 7864352 | tf_op jit(solution)/shard_map/ppermute | solution.py:18
  1086.3 32.0 %multiply_reduce_fusion = (f32[6144]{0:T(1024)S(1)}, f32[1536]{0:T(1024)S(1)}, f32[1536,6144]{1,0:T(8,128)}) fusion(f32[1536,6144]{1,0:T(8,128)} %fusion.14, bf16[512,7680]{0,1:T(8,128)(2,1)} %collective-permute-done.1), kind=kOutput, calls=%fused_computation.1 | convolution fusion | flops 9701416960 | bytes 83392512 | tf_op jit(solution)/shard_map/dot_general | solution.py:34
  1118.3 6.3 psum.21
  1124.7 0.7 fusion.31
  1125.3 17.4 %all-reduce = (f32[]{:T(128)}, f32[6144]{0:T(1024)S(1)}) all-reduce(f32[]{:T(128)} %get-tuple-element.6, f32[6144]{0:T(1024)S(1)} %get-tuple-element.2), channel_id=1, replica_groups=mesh['section'=2,'hid'=4,'wid'=4] {'hid'}, use_global_device_ids=true, to_apply=%region_7.8 | all-reduce | flops 6145 | bytes 49160 | tf_op jit(solution)/shard_map/psum | solution.py:87
  1143.3 0.0 copy-done.6
  1143.4 28.6 %multiply_bitcast_fusion = f32[1,1536,6144]{2,1,0:T(8,128)} fusion(f32[1536,6144]{1,0:T(8,128)} %get-tuple-element.8, f32[]{:T(128)S(6)} %div.9, f32[6144]{0:T(1024)S(1)} %multiply_add_fusion, f32[1536]{0:T(1024)S(1)} %get-tuple-element.7), kind=kLoop, calls=%fused_computation | loop fusion | flops 28311552 | bytes 75528192 | tf_op jit(solution)/shard_map/broadcast_in_dim | solution.py:91
  (2 shorter events, 0.0 us)
Async XLA Ops:
  7.2 25.5 %all-gather.5.cloned.1.call-start = ((), (), s32[]{:S(2)}) async-start(), calls=%async_computation.2 | async-start | bytes 1966080 | tf_op jit(solution)/shard_map/all_gather | solution.py:46
  7.2 408.5 %collective-permute-start = (bf16[1536,6144]{1,0:T(8,128)(2,1)}, bf16[1536,6144]{1,0:T(8,128)(2,1)}, u32[]{:S(2)}, u32[]{:S(2)}) collective-permute-start(bf16[1536,6144]{1,0:T(8,128)(2,1)} %bitcast.17), channel_id=1, source_target_pairs={{16,0},{0,16},{17,1},{1,17},{18,2},{2,18},{19,3},{3,19},{20,4},{4,... | collective-permute-start | bytes 56623112 | tf_op jit(solution)/shard_map/ppermute | solution.py:18
  12.2 636.2 %reduce-scatter.3.cloned.1.call-start = ((), (), s32[]{:S(2)}) async-start(), calls=%async_computation.3 | async-start | bytes 15728640 | tf_op jit(solution)/shard_map/reduce_scatter | solution.py:53
  435.9 1.0 copy-start.5
  435.9 2.0 copy-start.3
  435.9 235.6 %all-gather.9.cloned.1.call-start = ((), (), s32[]{:S(2)}) async-start(), calls=%async_computation.6 | async-start | bytes 1966080 | tf_op jit(solution)/shard_map/all_gather | solution.py:47
  437.8 233.7 %copy-start = (bf16[512,1536]{0,1:T(8,128)(2,1)S(1)}, bf16[512,1536]{0,1:T(8,128)(2,1)}, u32[]{:S(2)}) copy-start(bf16[512,1536]{0,1:T(8,128)(2,1)} %all-gather.5.cloned.1.call-done) | copy-start | bytes 4718596
  437.8 349.9 %all-gather.11.cloned.1.call-start = ((), (), s32[]{:S(2)}) async-start(), calls=%async_computation.7 | async-start | bytes 7864320 | tf_op jit(solution)/shard_map/all_gather | solution.py:49
  439.5 463.3 %all-gather.7.cloned.1.call-start = ((), (), s32[]{:S(2)}) async-start(), calls=%async_computation.4 | async-start | bytes 7864320 | tf_op jit(solution)/shard_map/all_gather | solution.py:60
  652.4 319.0 %reduce-scatter.5.cloned.1.call-start = ((), (), s32[]{:S(2)}) async-start(), calls=%async_computation.5 | async-start | bytes 3932160 | tf_op jit(solution)/shard_map/reduce_scatter | solution.py:62
  914.0 18.8 %copy-start.8 = (f32[1,1536]{1,0:T(1,128)S(1)}, f32[1,1536]{1,0:T(1,128)}, u32[]{:S(2)}) copy-start(f32[1,1536]{1,0:T(1,128)} %param.10) | copy-start | bytes 18436
  914.0 18.8 %copy-start.7 = (f32[1,6144]{1,0:T(1,128)S(1)}, f32[1,6144]{1,0:T(1,128)}, u32[]{:S(2)}) copy-start(f32[1,6144]{1,0:T(1,128)} %param.11) | copy-start | bytes 73732
  914.0 19.5 %copy-start.1 = (bf16[512,1536]{0,1:T(8,128)(2,1)S(1)}, bf16[512,1536]{0,1:T(8,128)(2,1)}, u32[]{:S(2)}) copy-start(bf16[512,1536]{0,1:T(8,128)(2,1)} %all-gather.5.cloned.1.call-done) | copy-start | bytes 4718596
  914.0 19.5 %copy-start.2 = (bf16[512,1536]{0,1:T(8,128)(2,1)S(1)}, bf16[512,1536]{0,1:T(8,128)(2,1)}, u32[]{:S(2)}) copy-start(bf16[512,1536]{0,1:T(8,128)(2,1)} %all-gather.9.cloned.1.call-done) | copy-start | bytes 4718596
  914.0 172.4 %collective-permute-start.1 = (bf16[512,7680]{0,1:T(8,128)(2,1)}, bf16[512,7680]{0,1:T(8,128)(2,1)}, u32[]{:S(2)}, u32[]{:S(2)}) collective-permute-start(bf16[512,7680]{0,1:T(8,128)(2,1)} %pad_maximum_fusion), channel_id=1, source_target_pairs={{16,0},{0,16},{17,1},{1,17},{18,2},{2,18},{19,3},{3,19},{20,4},{4,... | collective-permute-start | bytes 23592968 | tf_op jit(solution)/shard_map/ppermute | solution.py:18
  933.5 37.9 %copy-start.4 = (bf16[128,1536]{1,0:T(8,128)(2,1)S(1)}, bf16[128,1536]{1,0:T(8,128)(2,1)}, u32[]{:S(2)}) copy-start(bf16[128,1536]{1,0:T(8,128)(2,1)} %param.9) | copy-start | bytes 1179652
  973.5 169.9 %copy-start.6 = (f32[1,6144]{1,0:T(1,128)S(1)}, f32[1,6144]{1,0:T(1,128)}, u32[]{:S(2)}) copy-start(f32[1,6144]{1,0:T(1,128)} %broadcast_multiply_fusion) | copy-start | bytes 73732
Sparse Core Ops, SparseCore 0:
  12.3 20.3 all-gather.4
  436.0 212.3 reduce-scatter.2
  650.6 20.8 all-gather.8
  672.9 114.8 all-gather.10
  789.7 113.0 all-gather.6
  932.9 38.4 reduce-scatter.4
where the time goes:
time: 1180 us
  waiting for transfers between devices  991 us (84%)
  matrix products  89.5 us (8%)
  other arithmetic  48.4 us (4%)
  blocking collectives  23.7 us (2%)
  between operations  14.8 us (1%)
    ppermute x2, waiting for transfers between devices, from_behind(): return lax.ppermute(block, axis, route)  496 us
    reduce_scatter x1, waiting for transfers between devices, shards(): lax.psum_scatter(jnp.dot(grad_rows, down_tile, preferred_element_type=jnp...  209 us
    all_gather x1, waiting for transfers between devices, shards(): pre_grad = lax.all_gather(pre_share, 'hid', axis=0, tiled=True)  115 us
    all_gather x1, waiting for transfers between devices, shards(): pre_half = lax.all_gather(preact, 'hid', axis=0, tiled=True)  115 us
    dot_general x2, matrix products, contract(): lax.dot_general(left, right, (((0,), (0,)), ((), ())), preferred_element_...  53.1 us
    broadcast_in_dim x1, other arithmetic, shards(): return (input_grad, update[None])  28.6 us
  transfers between devices with their start and end apart: 8, of which 8 were waited for; matrix products, arithmetic and copies ran while one was open for 4% of the time, Pallas kernels for 0%

commit v1 on v0

v1 whole, which is shorter than its diff:
```python
import jax
import jax.numpy as jnp
from jax import lax
from jax.sharding import PartitionSpec as P

decay_rate = 0.9
root_half = 0.7071067811865476
inv_root_tau = 0.3989422804014327
LANES = 2
CUTS = 2


def normal_cdf(pre):
    return 0.5 * (1.0 + lax.erf(pre * root_half))


def gelu_value(pre):
    return pre * normal_cdf(pre)


def gelu_slope(pre):
    return normal_cdf(pre) + pre * jnp.exp(-0.5 * pre * pre) * inv_root_tau


def contract(left, right):
    return lax.dot_general(
        left, right, (((0,), (0,)), ((), ())), preferred_element_type=jnp.float32
    )


def chain_place(stream, pos, n):
    section, z = (1, pos) if pos < n else (0, 2 * n - 1 - pos)
    return section * n + (z if stream else n - 1 - z)


def shards(weights, preact, inputs, grad_out, row_state, col_state):
    n = lax.axis_size("hid")
    nw = lax.axis_size("wid")
    section = lax.axis_index("section")
    z = lax.axis_index("hid")
    w = lax.axis_index("wid")
    up = section == 0
    tile = weights[0]
    rows, width = preact.shape
    step_rows = rows // (LANES * CUTS)
    chunks = n * CUTS
    both = ("section", "hid")

    mine = jnp.where(up, inputs, grad_out)
    other = lax.ppermute(jnp.where(up, grad_out, inputs), "section", [(0, 1), (1, 0)])
    pair = jnp.stack([jnp.where(up, mine, other), jnp.where(up, other, mine)])
    left = lax.all_gather(pair, "wid", axis=1, tiled=True)
    depth = left.shape[-1]
    left = left.reshape(2, n, LANES, CUTS, step_rows, depth)
    halves = []
    for stream in (0, 1):
        order = range(n - 1, n // 2 - 1, -1) if stream else range(n // 2)
        picked = jnp.stack([left[s, k] for k in order for s in (1, 0)])
        halves.append(jnp.transpose(picked, (1, 0, 2, 3, 4)))
    left = jnp.stack(halves).reshape(-1, depth)
    part = jnp.dot(left, tile, preferred_element_type=jnp.float32)
    highest = jnp.where(up, 0.0, jnp.max(jnp.abs(part), axis=1))
    highest = lax.pmax(highest, "hid")
    scale = 16384.0 / jnp.maximum(n * highest, 1e-30)
    part = (part * scale[:, None]).astype(jnp.float16)
    part = part.reshape(2, LANES, chunks * step_rows, width)
    unscale = (1.0 / scale).reshape(2, LANES, chunks, step_rows, 1)

    total = 2 * LANES * chunks
    buf = jnp.zeros((total + 1, step_rows, width), jnp.bfloat16)

    def put_block(buf, block, s, at, valid):
        pieces = block.reshape(LANES, CUTS, step_rows, width)
        stream = at >= n // 2
        index = jnp.where(stream, n - 1 - at, at) * 2 + (1 - s)
        for lane in range(LANES):
            for cut in range(CUTS):
                base = (stream.astype(jnp.int32) * LANES + lane) * chunks + index * CUTS + cut
                slot = jnp.where(valid & (section == 1), base, total)
                buf = lax.dynamic_update_slice(buf, pieces[lane, cut][None], (slot, 0, 0))
        return buf

    def over_y(block):
        return lax.ppermute(block, "section", [(0, 1)])

    rightward = [(s * n + k, s * n + k + 1) for s in (0, 1) for k in range(n - 1)]
    leftward = [(b, a) for a, b in rightward]
    pre_own = preact
    pre_other = over_y(preact)
    pre_blocks = [[(pre_own, pre_other)], [(pre_own, pre_other)]]
    buf = put_block(buf, pre_own, 1, z, True)
    buf = put_block(buf, pre_other, 0, z, True)
    travel = [preact, preact]

    lanes = [(stream, lane) for stream in (0, 1) for lane in range(LANES)]
    pos = [
        jnp.where(up, 2 * n - 1 - (z if st else n - 1 - z), (z if st else n - 1 - z))
        for st in (0, 1)
    ]
    incoming = {key: None for key in lanes}
    carry = {key: None for key in lanes}

    def hops(st, places):
        return [(chain_place(st, q, n), chain_place(st, q + 1, n)) for q in places]

    ticks = chunks + 2 * n - 1
    spread = max(1, (chunks + n) // (n - 1)) if n > 1 else 1
    hop = 0
    for t in range(ticks):
        if hop < n - 1 and (t % spread == 0 or t == ticks - 1):
            hop += 1
            if carry[lanes[0]] is not None:
                tied = lax.optimization_barrier((travel, carry[lanes[0]]))
                travel, carry[lanes[0]] = list(tied[0]), tied[1]
            k = hop
            travel = [
                lax.ppermute(travel[0], both, [p for p in leftward if p[1] % n + k < n]),
                lax.ppermute(travel[1], both, [p for p in rightward if p[1] % n - k >= 0]),
            ]
            others = [over_y(block) for block in travel]
            for st in (0, 1):
                pre_blocks[st].append((travel[st], others[st]))
                at = z - k if st else z + k
                valid = (at >= 0) & (at < n)
                buf = put_block(buf, travel[st], 1, at, valid)
                buf = put_block(buf, others[st], 0, at, valid)
        for st, lane in lanes:
            got = incoming[st, lane]
            c = t - pos[st]
            if got is not None and t >= n:
                valid = up & (c >= 0) & (c < chunks)
                slot = jnp.where(valid, (st * LANES + lane) * chunks + c, total)
                buf = lax.dynamic_update_slice(buf, got[None], (slot, 0, 0))
            useful = [q for q in range(2 * n - 1) if 0 <= t - q < chunks]
            summing = [q for q in useful if q < n - 1]
            passing = [q for q in useful if q >= n - 1]
            at_end = t - (n - 1)
            sums = carry[st, lane]
            carry[st, lane] = incoming[st, lane] = None
            if summing or 0 <= at_end < chunks:
                start = jnp.clip(c, 0, chunks - 1) * step_rows
                value = lax.dynamic_slice(
                    part, (st, lane, start, 0), (1, 1, step_rows, width)
                )[0, 0].astype(jnp.float32)
                if sums is not None:
                    value = value + sums.astype(jnp.float32)
            if summing:
                carry[st, lane] = lax.ppermute(
                    value.astype(jnp.float16), both, hops(st, summing)
                )
            if passing:
                message = got
                if 0 <= at_end < chunks:
                    block, cut = divmod(at_end, CUTS)
                    pre = pre_blocks[st][block // 2][block % 2]
                    pre = pre.reshape(LANES, CUTS, step_rows, width)[lane, cut]
                    slope = gelu_slope(pre.astype(jnp.float32))
                    made = value * unscale[st, lane, at_end] * slope
                    message = made.astype(jnp.bfloat16)
                    if got is not None:
                        message = jnp.where(up, got, message)
                incoming[st, lane] = lax.ppermute(message, both, hops(st, passing))

    full = buf[:total].reshape(total * step_rows, width)

    share = lax.dot_general(
        full, tile, (((1,), (1,)), ((), ())), preferred_element_type=jnp.float32
    )
    share = share.reshape(2, LANES, n // 2, 2, CUTS, step_rows, depth)
    natural = [[None] * n, [None] * n]
    for stream in (0, 1):
        for i in range(n // 2):
            at = n - 1 - i if stream else i
            for j in (0, 1):
                natural[1 - j][at] = share[stream, :, i, j].reshape(rows, depth)
    share = jnp.stack([jnp.concatenate(half) for half in natural])
    tokens = grad_out.shape[0]
    share = share.reshape(2, nw, tokens, depth)
    summed = lax.dynamic_slice(share, (0, w, 0, 0), (2, 1, tokens, depth))[:, 0]
    wide = ("section", "wid")
    for d in range(1, nw):
        target = lax.rem(w + d, nw)
        out = lax.dynamic_slice(share, (0, target, 0, 0), (2, 1, tokens, depth))[:, 0]
        got = lax.ppermute(
            out.astype(jnp.bfloat16), wide, [(i, (i + d) % nw) for i in range(nw)]
        )
        summed = summed + got.astype(jnp.float32)
    across = lax.ppermute(summed[1], "section", [(0, 1)])
    input_grad = jnp.where(up, summed[0], across) + grad_out.astype(jnp.float32)

    right = jnp.where(up, full, gelu_value(full.astype(jnp.float32)).astype(jnp.bfloat16))
    gradient = contract(left, right)
    squares = gradient * gradient
    row_local = jnp.sum(squares, axis=1)
    col_local = jnp.sum(squares, axis=0)
    ff = width * nw
    d_model = depth * n
    row_total = lax.psum(row_local, "wid")
    row_moment = decay_rate * row_state[0] + (1.0 - decay_rate) / ff * row_total
    col_total, row_sum = lax.psum((col_local, jnp.sum(row_moment)), "hid")
    col_moment = decay_rate * col_state[0] + (1.0 - decay_rate) / d_model * col_total
    row_mean = row_sum / d_model
    update = gradient * lax.rsqrt(row_moment[:, None] * col_moment[None, :] / row_mean)
    return (input_grad, update[None])


def solution(mesh):
    placed = (
        P("section", "hid", "wid"),
        P(("section", "hid"), "wid"),
        P(("section", "wid"), "hid"),
        P(("section", "wid"), "hid"),
        P("section", "hid"),
        P("section", "wid"),
    )
    return jax.shard_map(
        shards,
        mesh=mesh,
        in_specs=placed,
        out_specs=(P(("section", "wid"), "hid"), P("section", "hid", "wid")),
        check_vma=False,
    )
```

time: 1180 us -> 929 us (0.79)
  waiting for transfers between devices: 991 us -> 218 us
  starting transfers between devices: 6.06 us -> 424 us
  other arithmetic: 48.4 us -> 95 us
  local copies, waits for them, and re-layouts: 5.35 us -> 44 us
  blocking collectives: 23.7 us -> 39.2 us
    ppermute x2 -> x102, starting transfers between devices: 5.63 us -> 424 us  [the longest x44 145 us: shards(): incoming[st, lane] = lax.ppermute(message, both, hops(st, passing))]
    ppermute x2 -> x102, waiting for transfers between devices: 496 us -> 192 us  [the longest x44 99.5 us: shards(): incoming[st, lane] = lax.ppermute(message, both, hops(st, passing))]
    all_gather x4 -> x1, waiting for transfers between devices: 269 us -> 26.1 us  [shards(): left = lax.all_gather(pair, 'wid', axis=1, tiled=True)]
    reduce_scatter x2 -> x0, waiting for transfers between devices: 226 us -> none  [the longest x1 209 us: shards(): lax.psum_scatter(jnp.dot(grad_rows, down_tile, preferred_element_type=jnp...]
    dynamic_update_slice x0 -> x100, local copies, waits for them, and re-layouts: none -> 30.4 us  [the longest x56 28.9 us: put_block(): buf = lax.dynamic_update_slice(buf, pieces[lane, cut][None], (slot, 0, 0))]
    dot_general x2 -> x1, matrix products: 53.1 us -> 28.3 us  [contract(): lax.dot_general(left, right, (((0,), (0,)), ((), ())), preferred_element_...]
    select_n x2 -> x15, other arithmetic: 7.37 us -> 31.5 us  [the longest x12 21.8 us: shards(): message = jnp.where(up, got, message)]
    convert_element_type x1 -> x27, other arithmetic: 3.93 us -> 25.4 us  [the longest x23 10.2 us: shards(): value.astype(jnp.float16)]
  transfers between devices with their start and end apart: 8 -> 103, of which waited for: 8 -> 23; matrix products, arithmetic and copies ran while one was open for 4% -> 19% of each run, Pallas kernels for 0% -> 0%
where the time goes in v1:
time: 929 us; the launch traced here: 918 us
  starting transfers between devices  424 us (46%)
  waiting for transfers between devices  218 us (23%)
  other arithmetic  95 us (10%)
  matrix products  79 us (9%)
  local copies, waits for them, and re-layouts  44 us (5%)
  blocking collectives  39.2 us (4%)
  between operations  18 us (2%)
    ppermute x44, starting transfers between devices, shards(): incoming[st, lane] = lax.ppermute(message, both, hops(st, passing))  145 us
    ppermute x40, starting transfers between devices, shards(): lax.ppermute(value.astype(jnp.float16), both, hops(st, summing))  123 us
    ppermute x44, waiting for transfers between devices, shards(): incoming[st, lane] = lax.ppermute(message, both, hops(st, passing))  99.5 us
    ppermute x7, waiting for transfers between devices, over_y(): return lax.ppermute(block, 'section', [(0, 1)])  79.1 us
    ppermute x7, starting transfers between devices, over_y(): return lax.ppermute(block, 'section', [(0, 1)])  76.7 us
    ppermute x3, starting transfers between devices, shards(): lax.ppermute(out.astype(jnp.bfloat16), wide, [(i, (i + d) % nw) for i in...  38.7 us
    dynamic_update_slice x56, local copies, waits for them, and re-layouts, put_block(): buf = lax.dynamic_update_slice(buf, pieces[lane, cut][None], (slot, 0, 0))  28.9 us
    broadcast_in_dim x1, other arithmetic, shards(): return (input_grad, update[None])  28.7 us
  transfers between devices with their start and end apart: 103, of which 23 were waited for; matrix products, arithmetic and copies ran while one was open for 19% of the time, Pallas kernels for 0%

profile of v1, /device:TPU:0, one launch (start us, length us, event | category | flops | bytes accessed | tf_op | source)
XLA Modules:
  0.0 917.5 jit_solution(14788876595519778440)
XLA Ops:
  7.2 5.1 collective-permute-start
  12.4 7.1 collective-permute-start.3
  19.4 4.6 collective-permute-start.1
  25.8 7.5 collective-permute-start.5
  33.3 6.3 broadcast_in_dim.145
  41.2 13.4 %collective-permute-done.5 = bf16[128,1536]{1,0:T(8,128)(2,1)} collective-permute-done((bf16[128,1536]{1,0:T(8,128)(2,1)}, bf16[128,1536]{1,0:T(8,128)(2,1)}, u32[]{:S(2)}, u32[]{:S(2)}) %collective-permute-start.5) | collective-permute-done | bytes 393248 | tf_op jit(solution)/shard_map/ppermute | solution.py:50
  61.5 26.1 %all-gather.2.cloned.1.call-done = bf16[2,512,1536]{2,1,0:T(8,128)(2,1)} async-done(((bf16[2,128,1536]{2,1,0:T(8,128)(2,1)}), bf16[2,512,1536]{2,1,0:T(8,128)(2,1)}) %all-gather.2.cloned.1.call-update) | async-done | bytes 3145744 | tf_op jit(solution)/shard_map/all_gather | solution.py:52
  90.1 26.6 %abs_reduce_fusion = (f32[1024]{0:T(1024)S(1)}, f32[1024,6144]{1,0:T(8,128)}) fusion(bf16[1024,1536]{1,0:T(8,128)(2,1)S(1)} %bitcast.831, bf16[1,1536,6144]{2,1,0:T(8,128)(2,1)} %param.6), kind=kOutput, calls=%fused_computation.10 | convolution fusion | flops 19339935744 | bytes 47190016 | tf_op jit(solution)/shard_map/dot_general | solution.py:61
  116.8 11.7 %pmax.7 = f32[1024]{0:T(1024)S(1)} all-reduce(f32[1024]{0:T(1024)S(1)} %broadcast_select_fusion.2), channel_id=1, replica_groups=mesh['section'=2,'hid'=4,'wid'=4] {'hid'}, use_global_device_ids=true, to_apply=%region_1.2 | all-reduce | flops 1024 | bytes 8192 | tf_op jit(solution)/shard_map/pmax | solution.py:63
  129.1 9.8 %multiply_convert_fusion = f16[1024,6144]{1,0:T(8,128)(2,1)S(1)} fusion(f32[1024,6144]{1,0:T(8,128)} %get-tuple-element.134, f32[1024]{0:T(1024)S(1)} %get-tuple-element.132), kind=kLoop, calls=%fused_computation.9 | loop fusion | flops 12582912 | bytes 37752832 | tf_op jit(solution)/shard_map/convert_element_type | solution.py:65
  162.2 54.4 %collective-permute-start.2 = (bf16[128,6144]{1,0:T(8,128)(2,1)}, bf16[128,6144]{1,0:T(8,128)(2,1)S(1)}, u32[]{:S(2)}, u32[]{:S(2)}) collective-permute-start(bf16[128,6144]{1,0:T(8,128)(2,1)} %collective-permute-done.1), channel_id=1, source_target_pairs={{0,16},{1,17},{2,18},{3,19},{4,20},{5,21},{6,22},{7,23},{8,24},{9,... | collective-permute-start | bytes 4718600 | tf_op jit(solution)/shard_map/ppermute | solution.py:84
  220.4 7.1 collective-permute-start.4
  230.7 20.9 %collective-permute-done.2 = bf16[128,6144]{1,0:T(8,128)(2,1)S(1)} collective-permute-done((bf16[128,6144]{1,0:T(8,128)(2,1)}, bf16[128,6144]{1,0:T(8,128)(2,1)S(1)}, u32[]{:S(2)}, u32[]{:S(2)}) %collective-permute-start.2) | collective-permute-done | bytes 1572896 | tf_op jit(solution)/shard_map/ppermute | solution.py:84
  273.1 6.4 collective-permute-done.4
  288.2 89.2 %collective-permute-start.76 = (f16[32,6144]{1,0:T(8,128)(2,1)S(1)}, f16[32,6144]{1,0:T(8,128)(2,1)S(1)}, u32[]{:S(2)}, u32[]{:S(2)}) collective-permute-start(f16[32,6144]{1,0:T(8,128)(2,1)S(1)} %get-tuple-element.61), channel_id=1, source_target_pairs={{20,24},{24,28},{21,25},{25,29},{22,26},{26,30},{23,27},{27,31}} | collective-permute-start | bytes 1179656 | tf_op jit(solution)/shard_map/ppermute | solution.py:148
  377.4 6.3 collective-permute-start.74
  386.6 10.5 %collective-permute-start.33 = (bf16[32,6144]{1,0:T(8,128)(2,1)S(1)}, bf16[32,6144]{1,0:T(8,128)(2,1)S(1)}, u32[]{:S(2)}, u32[]{:S(2)}) collective-permute-start(bf16[32,6144]{1,0:T(8,128)(2,1)S(1)} %get-tuple-element.43), channel_id=1, source_target_pairs={{28,12},{12,8},{29,13},{13,9},{30,14},{14,10},{31,15},{15,11}} | collective-permute-start | bytes 1179656 | tf_op jit(solution)/shard_map/ppermute | solution.py:162
  397.2 3.8 collective-permute-start.29
  401.0 3.9 collective-permute-start.31
  409.7 12.1 %collective-permute-done.14 = bf16[32,6144]{1,0:T(8,128)(2,1)S(1)} collective-permute-done((bf16[32,6144]{1,0:T(8,128)(2,1)S(1)}, bf16[32,6144]{1,0:T(8,128)(2,1)S(1)}, u32[]{:S(2)}, u32[]{:S(2)}) %collective-permute-start.14) | collective-permute-done | bytes 393248 | tf_op jit(solution)/shard_map/ppermute | solution.py:162
  424.0 12.5 %collective-permute-start.27 = (bf16[32,6144]{1,0:T(8,128)(2,1)S(1)}, bf16[32,6144]{1,0:T(8,128)(2,1)S(1)}, u32[]{:S(2)}, u32[]{:S(2)}) collective-permute-start(bf16[32,6144]{1,0:T(8,128)(2,1)S(1)} %get-tuple-element.71), channel_id=1, source_target_pairs={{16,0},{0,4},{17,1},{1,5},{18,2},{2,6},{19,3},{3,7}} | collective-permute-start | bytes 1179656 | tf_op jit(solution)/shard_map/ppermute | solution.py:162
  438.6 5.8 collective-permute-start.10
  444.5 6.7 collective-permute-start.12
  454.1 8.0 collective-permute-start.35
  462.3 28.9 %collective-permute-done.49 = bf16[32,6144]{1,0:T(8,128)(2,1)S(1)} collective-permute-done((bf16[32,6144]{1,0:T(8,128)(2,1)S(1)}, bf16[32,6144]{1,0:T(8,128)(2,1)S(1)}, u32[]{:S(2)}, u32[]{:S(2)}) %collective-permute-start.49) | collective-permute-done | bytes 393248 | tf_op jit(solution)/shard_map/ppermute | solution.py:162
  494.8 9.2 collective-permute-start.37
  503.9 3.5 collective-permute-done.62
  515.9 4.7 collective-permute-done.60
  525.3 4.6 collective-permute-start.45
  531.4 5.5 collective-permute-done.69
  538.9 6.5 collective-permute-done.45
  548.6 4.4 collective-permute-start.58
  555.4 4.5 collective-permute-done.58
  565.3 6.5 collective-permute-start.56
  575.9 7.1 collective-permute-done.75
  583.1 4.5 collective-permute-start.54
  587.5 3.9 collective-permute-start.13
  591.5 3.4 fusion.300
  594.9 3.4 collective-permute-start.65
  598.7 26.6 %collective-permute-done.13 = bf16[128,6144]{1,0:T(8,128)(2,1)S(1)} collective-permute-done((bf16[128,6144]{1,0:T(8,128)(2,1)S(1)}, bf16[128,6144]{1,0:T(8,128)(2,1)S(1)}, u32[]{:S(2)}, u32[]{:S(2)}) %collective-permute-start.13) | collective-permute-done | bytes 1572896 | tf_op jit(solution)/shard_map/ppermute | solution.py:84
  625.3 3.4 collective-permute-start.63
  630.2 7.4 collective-permute-done.63
  641.3 5.2 collective-permute-start.73
  646.5 4.8 collective-permute-start.71
  653.2 4.5 collective-permute-done.83
  657.7 9.0 collective-permute-start.89
  666.7 6.4 collective-permute-start.88
  674.2 4.4 collective-permute-start.81
  678.6 3.4 collective-permute-start.79
  683.4 4.2 collective-permute-done.88
  688.8 5.9 collective-permute-start.87
  695.9 6.6 collective-permute-start.86
  708.4 4.2 collective-permute-done.86
  714.5 25.1 %collective-permute-done.55 = bf16[128,6144]{1,0:T(8,128)(2,1)S(1)} collective-permute-done((bf16[128,6144]{1,0:T(8,128)(2,1)S(1)}, bf16[128,6144]{1,0:T(8,128)(2,1)S(1)}, u32[]{:S(2)}, u32[]{:S(2)}) %collective-permute-start.55) | collective-permute-done | bytes 1572896 | tf_op jit(solution)/shard_map/ppermute | solution.py:84
  742.4 7.9 fusion.4
  750.2 24.1 %fusion.5 = f32[2,2,2,2,2,32,1536]{6,5,4,3,2,1,0:T(8,128)S(1)} fusion(bf16[2,2,2,2,2,32,6144]{6,5,4,3,2,1,0:T(8,128)(2,1)} %bitcast.802, bf16[1,1536,6144]{2,1,0:T(8,128)(2,1)} %param.6), kind=kOutput, calls=%fused_computation.12 | convolution fusion | flops 19327352832 | bytes 37748736 | tf_op jit(solution)/shard_map/dot_general | solution.py:166
  778.6 23.9 %collective-permute-start.98 = (bf16[2,128,1536]{2,1,0:T(8,128)(2,1)}, bf16[2,128,1536]{2,1,0:T(8,128)(2,1)}, u32[]{:S(2)}, u32[]{:S(2)}) collective-permute-start(bf16[2,128,1536]{2,1,0:T(8,128)(2,1)} %get-tuple-element.78), channel_id=1, source_target_pairs={{0,1},{1,2},{2,3},{3,0},{4,5},{5,6},{6,7},{7,4},{8,9},{9,10},{10,1... | collective-permute-start | bytes 2359304 | tf_op jit(solution)/shard_map/ppermute | solution.py:184
  802.6 7.2 collective-permute-start.99
  809.8 7.5 collective-permute-start.100
  817.4 28.3 %multiply_reduce_fusion = (f32[6144]{0:T(1024)S(1)}, f32[1536]{0:T(1024)S(1)}, f32[1536,6144]{1,0:T(8,128)}) fusion(bf16[1024,1536]{1,0:T(8,128)(2,1)} %bitcast.832, bf16[1024,6144]{1,0:T(8,128)(2,1)S(1)} %bitcast.801), kind=kOutput, calls=%fused_computation.1 | convolution fusion | flops 19355656192 | bytes 53508096 | tf_op jit(solution)/shard_map/dot_general | solution.py:26
  845.7 7.4 psum.21
  853.7 20.1 %all-reduce = (f32[]{:T(128)}, f32[6144]{0:T(1024)S(1)}) all-reduce(f32[]{:T(128)} %get-tuple-element.18, f32[6144]{0:T(1024)S(1)} %get-tuple-element.14), channel_id=1, replica_groups=mesh['section'=2,'hid'=4,'wid'=4] {'hid'}, use_global_device_ids=true, to_apply=%region_7.8 | all-reduce | flops 6145 | bytes 49160 | tf_op jit(solution)/shard_map/psum | solution.py:200
  876.8 3.7 collective-permute-start.101
  880.6 28.7 %multiply_bitcast_fusion = f32[1,1536,6144]{2,1,0:T(8,128)} fusion(f32[1536,6144]{1,0:T(8,128)} %get-tuple-element.135, f32[]{:T(128)S(6)} %div.25, f32[6144]{0:T(1024)S(1)} %multiply_add_fusion, f32[1536]{0:T(1024)S(1)} %get-tuple-element.19), kind=kLoop, calls=%fused_computation | loop fusion | flops 28311552 | bytes 75528192 | tf_op jit(solution)/shard_map/broadcast_in_dim | solution.py:204
  (365 shorter events, 153.2 us)
Async XLA Ops:
  7.2 80.4 %all-gather.2.cloned.1.call-start = ((), (), s32[]{:S(2)}) async-start(), calls=%async_computation | async-start | bytes 3932160 | tf_op jit(solution)/shard_map/all_gather | solution.py:52
  7.2 53.4 %collective-permute-start = (bf16[128,6144]{1,0:T(8,128)(2,1)}, bf16[128,6144]{1,0:T(8,128)(2,1)S(1)}, u32[]{:S(2)}, u32[]{:S(2)}) collective-permute-start(bf16[128,6144]{1,0:T(8,128)(2,1)} %param.7), channel_id=1, source_target_pairs={{0,16},{1,17},{2,18},{3,19},{4,20},{5,21},{6,22},{7,23},{8,24},{9,... | collective-permute-start | bytes 4718600 | tf_op jit(solution)/shard_map/ppermute | solution.py:84
  12.4 208.0 %collective-permute-start.3 = (bf16[128,6144]{1,0:T(8,128)(2,1)}, bf16[128,6144]{1,0:T(8,128)(2,1)}, u32[]{:S(2)}, u32[]{:S(2)}) collective-permute-start(bf16[128,6144]{1,0:T(8,128)(2,1)} %param.7), channel_id=1, source_target_pairs={{0,4},{4,8},{8,12},{16,20},{20,24},{24,28},{1,5},{5,9},{9,13},{17,... | collective-permute-start | bytes 4718600 | tf_op jit(solution)/shard_map/ppermute | solution.py:118
  19.4 130.8 %collective-permute-start.1 = (bf16[128,6144]{1,0:T(8,128)(2,1)}, bf16[128,6144]{1,0:T(8,128)(2,1)}, u32[]{:S(2)}, u32[]{:S(2)}) collective-permute-start(bf16[128,6144]{1,0:T(8,128)(2,1)} %param.7), channel_id=1, source_target_pairs={{4,0},{8,4},{12,8},{20,16},{24,20},{28,24},{5,1},{9,5},{13,9},{21,... | collective-permute-start | bytes 4718600 | tf_op jit(solution)/shard_map/ppermute | solution.py:117
  25.8 28.8 %collective-permute-start.5 = (bf16[128,1536]{1,0:T(8,128)(2,1)}, bf16[128,1536]{1,0:T(8,128)(2,1)}, u32[]{:S(2)}, u32[]{:S(2)}) collective-permute-start(bf16[128,1536]{1,0:T(8,128)(2,1)} %broadcast_select_fusion), channel_id=1, source_target_pairs={{0,16},{16,0},{1,17},{17,1},{2,18},{18,2},{3,19},{19,3},{4,20},{20... | collective-permute-start | bytes 1179656 | tf_op jit(solution)/shard_map/ppermute | solution.py:50
  159.7 56.9 %collective-permute-start.40 = (f16[32,6144]{1,0:T(8,128)(2,1)S(1)}, f16[32,6144]{1,0:T(8,128)(2,1)S(1)}, u32[]{:S(2)}, u32[]{:S(2)}) collective-permute-start(f16[32,6144]{1,0:T(8,128)(2,1)S(1)} %fusion.220), channel_id=1, source_target_pairs={{16,20},{20,24},{24,28},{17,21},{21,25},{25,29},{18,22},{22,26},{2... | collective-permute-start | bytes 1179656 | tf_op jit(solution)/shard_map/ppermute | solution.py:148
  162.2 89.5 %collective-permute-start.2 = (bf16[128,6144]{1,0:T(8,128)(2,1)}, bf16[128,6144]{1,0:T(8,128)(2,1)S(1)}, u32[]{:S(2)}, u32[]{:S(2)}) collective-permute-start(bf16[128,6144]{1,0:T(8,128)(2,1)} %collective-permute-done.1), channel_id=1, source_target_pairs={{0,16},{1,17},{2,18},{3,19},{4,20},{5,21},{6,22},{7,23},{8,24},{9,... | collective-permute-start | bytes 4718600 | tf_op jit(solution)/shard_map/ppermute | solution.py:84
  220.4 59.2 %collective-permute-start.4 = (bf16[128,6144]{1,0:T(8,128)(2,1)}, bf16[128,6144]{1,0:T(8,128)(2,1)S(1)}, u32[]{:S(2)}, u32[]{:S(2)}) collective-permute-start(bf16[128,6144]{1,0:T(8,128)(2,1)} %collective-permute-done.3), channel_id=1, source_target_pairs={{0,16},{1,17},{2,18},{3,19},{4,20},{5,21},{6,22},{7,23},{8,24},{9,... | collective-permute-start | bytes 4718600 | tf_op jit(solution)/shard_map/ppermute | solution.py:84
  227.5 24.9 %collective-permute-start.15 = (f16[32,6144]{1,0:T(8,128)(2,1)}, f16[32,6144]{1,0:T(8,128)(2,1)S(1)}, u32[]{:S(2)}, u32[]{:S(2)}) collective-permute-start(f16[32,6144]{1,0:T(8,128)(2,1)} %get-tuple-element.72), channel_id=1, source_target_pairs={{28,24},{29,25},{30,26},{31,27}} | collective-permute-start | bytes 1179656 | tf_op jit(solution)/shard_map/ppermute | solution.py:148
  228.2 24.3 %collective-permute-start.30 = (f16[32,6144]{1,0:T(8,128)(2,1)S(1)}, f16[32,6144]{1,0:T(8,128)(2,1)S(1)}, u32[]{:S(2)}, u32[]{:S(2)}) collective-permute-start(f16[32,6144]{1,0:T(8,128)(2,1)S(1)} %get-tuple-element.48), channel_id=1, source_target_pairs={{16,20},{20,24},{24,28},{17,21},{21,25},{25,29},{18,22},{22,26},{2... | collective-permute-start | bytes 1179656 | tf_op jit(solution)/shard_map/ppermute | solution.py:148
  230.0 22.4 %collective-permute-start.61 = (f16[32,6144]{1,0:T(8,128)(2,1)S(1)}, f16[32,6144]{1,0:T(8,128)(2,1)S(1)}, u32[]{:S(2)}, u32[]{:S(2)}) collective-permute-start(f16[32,6144]{1,0:T(8,128)(2,1)S(1)} %fusion.228), channel_id=1, source_target_pairs={{16,20},{20,24},{24,28},{17,21},{21,25},{25,29},{18,22},{22,26},{2... | collective-permute-start | bytes 1179656 | tf_op jit(solution)/shard_map/ppermute | solution.py:148
  282.9 94.5 %collective-permute-start.7 = (f16[32,6144]{1,0:T(8,128)(2,1)S(1)}, f16[32,6144]{1,0:T(8,128)(2,1)S(1)}, u32[]{:S(2)}, u32[]{:S(2)}) collective-permute-start(f16[32,6144]{1,0:T(8,128)(2,1)S(1)} %get-tuple-element.64), channel_id=1, source_target_pairs={{28,24},{24,20},{29,25},{25,21},{30,26},{26,22},{31,27},{27,23}} | collective-permute-start | bytes 1179656 | tf_op jit(solution)/shard_map/ppermute | solution.py:148
  285.0 98.9 %collective-permute-start.26 = (bf16[32,6144]{1,0:T(8,128)(2,1)S(1)}, bf16[32,6144]{1,0:T(8,128)(2,1)S(1)}, u32[]{:S(2)}, u32[]{:S(2)}) collective-permute-start(bf16[32,6144]{1,0:T(8,128)(2,1)S(1)} %get-tuple-element.20), channel_id=1, source_target_pairs={{28,12},{29,13},{30,14},{31,15}} | collective-permute-start | bytes 1179656 | tf_op jit(solution)/shard_map/ppermute | solution.py:162
  285.9 98.8 %collective-permute-start.22 = (bf16[32,6144]{1,0:T(8,128)(2,1)S(1)}, bf16[32,6144]{1,0:T(8,128)(2,1)S(1)}, u32[]{:S(2)}, u32[]{:S(2)}) collective-permute-start(bf16[32,6144]{1,0:T(8,128)(2,1)S(1)} %get-tuple-element.46), channel_id=1, source_target_pairs={{28,12},{29,13},{30,14},{31,15}} | collective-permute-start | bytes 1179656 | tf_op jit(solution)/shard_map/ppermute | solution.py:162
  286.7 98.6 %collective-permute-start.18 = (bf16[32,6144]{1,0:T(8,128)(2,1)S(1)}, bf16[32,6144]{1,0:T(8,128)(2,1)S(1)}, u32[]{:S(2)}, u32[]{:S(2)}) collective-permute-start(bf16[32,6144]{1,0:T(8,128)(2,1)S(1)} %get-tuple-element.53), channel_id=1, source_target_pairs={{16,0},{17,1},{18,2},{19,3}} | collective-permute-start | bytes 1179656 | tf_op jit(solution)/shard_map/ppermute | solution.py:162
  288.2 108.9 %collective-permute-start.76 = (f16[32,6144]{1,0:T(8,128)(2,1)S(1)}, f16[32,6144]{1,0:T(8,128)(2,1)S(1)}, u32[]{:S(2)}, u32[]{:S(2)}) collective-permute-start(f16[32,6144]{1,0:T(8,128)(2,1)S(1)} %get-tuple-element.61), channel_id=1, source_target_pairs={{20,24},{24,28},{21,25},{25,29},{22,26},{26,30},{23,27},{27,31}} | collective-permute-start | bytes 1179656 | tf_op jit(solution)/shard_map/ppermute | solution.py:148
  377.4 23.5 %collective-permute-start.74 = (f16[32,6144]{1,0:T(8,128)(2,1)S(1)}, f16[32,6144]{1,0:T(8,128)(2,1)S(1)}, u32[]{:S(2)}, u32[]{:S(2)}) collective-permute-start(f16[32,6144]{1,0:T(8,128)(2,1)S(1)} %get-tuple-element.62), channel_id=1, source_target_pairs={{20,24},{24,28},{21,25},{25,29},{22,26},{26,30},{23,27},{27,31}} | collective-permute-start | bytes 1179656 | tf_op jit(solution)/shard_map/ppermute | solution.py:148
  383.9 21.0 %collective-permute-start.72 = (f16[32,6144]{1,0:T(8,128)(2,1)S(1)}, f16[32,6144]{1,0:T(8,128)(2,1)S(1)}, u32[]{:S(2)}, u32[]{:S(2)}) collective-permute-start(f16[32,6144]{1,0:T(8,128)(2,1)S(1)} %get-tuple-element.63), channel_id=1, source_target_pairs={{24,20},{20,16},{25,21},{21,17},{26,22},{22,18},{27,23},{23,19}} | collective-permute-start | bytes 1179656 | tf_op jit(solution)/shard_map/ppermute | solution.py:148
  384.6 20.3 %collective-permute-start.8 = (f16[32,6144]{1,0:T(8,128)(2,1)S(1)}, f16[32,6144]{1,0:T(8,128)(2,1)S(1)}, u32[]{:S(2)}, u32[]{:S(2)}) collective-permute-start(f16[32,6144]{1,0:T(8,128)(2,1)S(1)} %fusion.193), channel_id=1, source_target_pairs={{28,24},{24,20},{20,16},{29,25},{25,21},{21,17},{30,26},{26,22},{2... | collective-permute-start | bytes 1179656 | tf_op jit(solution)/shard_map/ppermute | solution.py:148
  386.6 23.1 %collective-permute-start.33 = (bf16[32,6144]{1,0:T(8,128)(2,1)S(1)}, bf16[32,6144]{1,0:T(8,128)(2,1)S(1)}, u32[]{:S(2)}, u32[]{:S(2)}) collective-permute-start(bf16[32,6144]{1,0:T(8,128)(2,1)S(1)} %get-tuple-element.43), channel_id=1, source_target_pairs={{28,12},{12,8},{29,13},{13,9},{30,14},{14,10},{31,15},{15,11}} | collective-permute-start | bytes 1179656 | tf_op jit(solution)/shard_map/ppermute | solution.py:162
  397.2 41.4 %collective-permute-start.29 = (bf16[32,6144]{1,0:T(8,128)(2,1)S(1)}, bf16[32,6144]{1,0:T(8,128)(2,1)S(1)}, u32[]{:S(2)}, u32[]{:S(2)}) collective-permute-start(bf16[32,6144]{1,0:T(8,128)(2,1)S(1)} %get-tuple-element.44), channel_id=1, source_target_pairs={{16,0},{0,4},{17,1},{1,5},{18,2},{2,6},{19,3},{3,7}} | collective-permute-start | bytes 1179656 | tf_op jit(solution)/shard_map/ppermute | solution.py:162
  423.3 21.1 %collective-permute-start.41 = (bf16[32,6144]{1,0:T(8,128)(2,1)S(1)}, bf16[32,6144]{1,0:T(8,128)(2,1)S(1)}, u32[]{:S(2)}, u32[]{:S(2)}) collective-permute-start(bf16[32,6144]{1,0:T(8,128)(2,1)S(1)} %get-tuple-element.40), channel_id=1, source_target_pairs={{28,12},{12,8},{8,4},{29,13},{13,9},{9,5},{30,14},{14,10},{10,6},{... | collective-permute-start | bytes 1179656 | tf_op jit(solution)/shard_map/ppermute | solution.py:162
  424.0 27.2 %collective-permute-start.27 = (bf16[32,6144]{1,0:T(8,128)(2,1)S(1)}, bf16[32,6144]{1,0:T(8,128)(2,1)S(1)}, u32[]{:S(2)}, u32[]{:S(2)}) collective-permute-start(bf16[32,6144]{1,0:T(8,128)(2,1)S(1)} %get-tuple-element.71), channel_id=1, source_target_pairs={{16,0},{0,4},{17,1},{1,5},{18,2},{2,6},{19,3},{3,7}} | collective-permute-start | bytes 1179656 | tf_op jit(solution)/shard_map/ppermute | solution.py:162
  437.3 57.5 %collective-permute-start.47 = (bf16[32,6144]{1,0:T(8,128)(2,1)S(1)}, bf16[32,6144]{1,0:T(8,128)(2,1)S(1)}, u32[]{:S(2)}, u32[]{:S(2)}) collective-permute-start(bf16[32,6144]{1,0:T(8,128)(2,1)S(1)} %get-tuple-element.39), channel_id=1, source_target_pairs={{28,12},{12,8},{8,4},{4,0},{29,13},{13,9},{9,5},{5,1},{30,14},{14,... | collective-permute-start | bytes 1179656 | tf_op jit(solution)/shard_map/ppermute | solution.py:162
  438.6 86.7 %collective-permute-start.10 = (bf16[128,6144]{1,0:T(8,128)(2,1)}, bf16[128,6144]{1,0:T(8,128)(2,1)S(1)}, u32[]{:S(2)}, u32[]{:S(2)}) collective-permute-start(bf16[128,6144]{1,0:T(8,128)(2,1)} %collective-permute-done.1), channel_id=1, source_target_pairs={{4,0},{8,4},{20,16},{24,20},{5,1},{9,5},{21,17},{25,21},{6,2},{10,... | collective-permute-start | bytes 4718600 | tf_op jit(solution)/shard_map/ppermute | solution.py:117
  444.5 85.4 %collective-permute-start.12 = (bf16[128,6144]{1,0:T(8,128)(2,1)}, bf16[128,6144]{1,0:T(8,128)(2,1)S(1)}, u32[]{:S(2)}, u32[]{:S(2)}) collective-permute-start(bf16[128,6144]{1,0:T(8,128)(2,1)} %collective-permute-done.3), channel_id=1, source_target_pairs={{4,8},{8,12},{20,24},{24,28},{5,9},{9,13},{21,25},{25,29},{6,10},{... | collective-permute-start | bytes 4718600 | tf_op jit(solution)/shard_map/ppermute | solution.py:118
  452.8 38.3 %collective-permute-start.49 = (bf16[32,6144]{1,0:T(8,128)(2,1)S(1)}, bf16[32,6144]{1,0:T(8,128)(2,1)S(1)}, u32[]{:S(2)}, u32[]{:S(2)}) collective-permute-start(bf16[32,6144]{1,0:T(8,128)(2,1)S(1)} %get-tuple-element.36), channel_id=1, source_target_pairs={{28,12},{12,8},{8,4},{4,0},{29,13},{13,9},{9,5},{5,1},{30,14},{14,... | collective-permute-start | bytes 1179656 | tf_op jit(solution)/shard_map/ppermute | solution.py:162
  454.1 57.6 %collective-permute-start.35 = (bf16[32,6144]{1,0:T(8,128)(2,1)S(1)}, bf16[32,6144]{1,0:T(8,128)(2,1)S(1)}, u32[]{:S(2)}, u32[]{:S(2)}) collective-permute-start(bf16[32,6144]{1,0:T(8,128)(2,1)S(1)} %get-tuple-element.37), channel_id=1, source_target_pairs={{16,0},{0,4},{4,8},{17,1},{1,5},{5,9},{18,2},{2,6},{6,10},{19,3},{... | collective-permute-start | bytes 1179656 | tf_op jit(solution)/shard_map/ppermute | solution.py:162
  494.8 20.5 %collective-permute-start.37 = (bf16[32,6144]{1,0:T(8,128)(2,1)S(1)}, bf16[32,6144]{1,0:T(8,128)(2,1)S(1)}, u32[]{:S(2)}, u32[]{:S(2)}) collective-permute-start(bf16[32,6144]{1,0:T(8,128)(2,1)S(1)} %get-tuple-element.38), channel_id=1, source_target_pairs={{16,0},{0,4},{4,8},{17,1},{1,5},{5,9},{18,2},{2,6},{6,10},{19,3},{... | collective-permute-start | bytes 1179656 | tf_op jit(solution)/shard_map/ppermute | solution.py:162
  511.7 52.4 %collective-permute-start.84 = (f16[32,6144]{1,0:T(8,128)(2,1)}, f16[32,6144]{1,0:T(8,128)(2,1)S(1)}, u32[]{:S(2)}, u32[]{:S(2)}) collective-permute-start(f16[32,6144]{1,0:T(8,128)(2,1)} %get-tuple-element.57), channel_id=1, source_target_pairs={{24,28},{25,29},{26,30},{27,31}} | collective-permute-start | bytes 1179656 | tf_op jit(solution)/shard_map/ppermute | solution.py:148
  515.2 57.5 %collective-permute-start.82 = (f16[32,6144]{1,0:T(8,128)(2,1)}, f16[32,6144]{1,0:T(8,128)(2,1)S(1)}, u32[]{:S(2)}, u32[]{:S(2)}) collective-permute-start(f16[32,6144]{1,0:T(8,128)(2,1)} %get-tuple-element.58), channel_id=1, source_target_pairs={{24,28},{25,29},{26,30},{27,31}} | collective-permute-start | bytes 1179656 | tf_op jit(solution)/shard_map/ppermute | solution.py:148
  525.3 20.1 %collective-permute-start.45 = (bf16[32,6144]{1,0:T(8,128)(2,1)S(1)}, bf16[32,6144]{1,0:T(8,128)(2,1)S(1)}, u32[]{:S(2)}, u32[]{:S(2)}) collective-permute-start(bf16[32,6144]{1,0:T(8,128)(2,1)S(1)} %get-tuple-element.41), channel_id=1, source_target_pairs={{16,0},{0,4},{4,8},{8,12},{17,1},{1,5},{5,9},{9,13},{18,2},{2,6},{... | collective-permute-start | bytes 1179656 | tf_op jit(solution)/shard_map/ppermute | solution.py:162
  529.9 16.2 %collective-permute-start.67 = (bf16[32,6144]{1,0:T(8,128)(2,1)S(1)}, bf16[32,6144]{1,0:T(8,128)(2,1)S(1)}, u32[]{:S(2)}, u32[]{:S(2)}) collective-permute-start(bf16[32,6144]{1,0:T(8,128)(2,1)S(1)} %get-tuple-element.68), channel_id=1, source_target_pairs={{28,12},{12,8},{8,4},{4,0},{29,13},{13,9},{9,5},{5,1},{30,14},{14,... | collective-permute-start | bytes 1179656 | tf_op jit(solution)/shard_map/ppermute | solution.py:162
  537.0 16.8 %collective-permute-start.43 = (bf16[32,6144]{1,0:T(8,128)(2,1)S(1)}, bf16[32,6144]{1,0:T(8,128)(2,1)S(1)}, u32[]{:S(2)}, u32[]{:S(2)}) collective-permute-start(bf16[32,6144]{1,0:T(8,128)(2,1)S(1)} %get-tuple-element.42), channel_id=1, source_target_pairs={{16,0},{0,4},{4,8},{8,12},{17,1},{1,5},{5,9},{9,13},{18,2},{2,6},{... | collective-permute-start | bytes 1179656 | tf_op jit(solution)/shard_map/ppermute | solution.py:162
  545.4 20.0 %collective-permute-start.70 = (f16[32,6144]{1,0:T(8,128)(2,1)S(1)}, f16[32,6144]{1,0:T(8,128)(2,1)S(1)}, u32[]{:S(2)}, u32[]{:S(2)}) collective-permute-start(f16[32,6144]{1,0:T(8,128)(2,1)S(1)} %fusion.233), channel_id=1, source_target_pairs={{24,20},{20,16},{25,21},{21,17},{26,22},{22,18},{27,23},{23,19}} | collective-permute-start | bytes 1179656 | tf_op jit(solution)/shard_map/ppermute | solution.py:148
  553.8 41.1 %collective-permute-start.11 = (bf16[128,6144]{1,0:T(8,128)(2,1)S(1)}, bf16[128,6144]{1,0:T(8,128)(2,1)S(1)}, u32[]{:S(2)}, u32[]{:S(2)}) collective-permute-start(bf16[128,6144]{1,0:T(8,128)(2,1)S(1)} %collective-permute-done.10), channel_id=1, source_target_pairs={{0,16},{1,17},{2,18},{3,19},{4,20},{5,21},{6,22},{7,23},{8,24},{9,... | collective-permute-start | bytes 4718600 | tf_op jit(solution)/shard_map/ppermute | solution.py:84
  564.0 19.0 %collective-permute-start.75 = (bf16[32,6144]{1,0:T(8,128)(2,1)S(1)}, bf16[32,6144]{1,0:T(8,128)(2,1)S(1)}, u32[]{:S(2)}, u32[]{:S(2)}) collective-permute-start(bf16[32,6144]{1,0:T(8,128)(2,1)S(1)} %get-tuple-element.29), channel_id=1, source_target_pairs={{28,12},{12,8},{8,4},{4,0},{29,13},{13,9},{9,5},{5,1},{30,14},{14,... | collective-permute-start | bytes 1179656 | tf_op jit(solution)/shard_map/ppermute | solution.py:162
  565.3 22.2 %collective-permute-start.56 = (bf16[32,6144]{1,0:T(8,128)(2,1)S(1)}, bf16[32,6144]{1,0:T(8,128)(2,1)S(1)}, u32[]{:S(2)}, u32[]{:S(2)}) collective-permute-start(bf16[32,6144]{1,0:T(8,128)(2,1)S(1)} %get-tuple-element.35), channel_id=1, source_target_pairs={{16,0},{0,4},{4,8},{8,12},{17,1},{1,5},{5,9},{9,13},{18,2},{2,6},{... | collective-permute-start | bytes 1179656 | tf_op jit(solution)/shard_map/ppermute | solution.py:162
  572.8 68.6 %collective-permute-start.80 = (f16[32,6144]{1,0:T(8,128)(2,1)}, f16[32,6144]{1,0:T(8,128)(2,1)S(1)}, u32[]{:S(2)}, u32[]{:S(2)}) collective-permute-start(f16[32,6144]{1,0:T(8,128)(2,1)} %get-tuple-element.59), channel_id=1, source_target_pairs={{20,16},{21,17},{22,18},{23,19}} | collective-permute-start | bytes 1179656 | tf_op jit(solution)/shard_map/ppermute | solution.py:148
  574.6 65.3 %collective-permute-start.52 = (bf16[128,6144]{1,0:T(8,128)(2,1)S(1)}, bf16[128,6144]{1,0:T(8,128)(2,1)S(1)}, u32[]{:S(2)}, u32[]{:S(2)}) collective-permute-start(bf16[128,6144]{1,0:T(8,128)(2,1)S(1)} %collective-permute-done.10), channel_id=1, source_target_pairs={{4,0},{20,16},{5,1},{21,17},{6,2},{22,18},{7,3},{23,19}} | collective-permute-start | bytes 4718600 | tf_op jit(solution)/shard_map/ppermute | solution.py:117
  583.1 95.6 %collective-permute-start.54 = (bf16[128,6144]{1,0:T(8,128)(2,1)S(1)}, bf16[128,6144]{1,0:T(8,128)(2,1)S(1)}, u32[]{:S(2)}, u32[]{:S(2)}) collective-permute-start(bf16[128,6144]{1,0:T(8,128)(2,1)S(1)} %collective-permute-done.12), channel_id=1, source_target_pairs={{8,12},{24,28},{9,13},{25,29},{10,14},{26,30},{11,15},{27,31}} | collective-permute-start | bytes 4718600 | tf_op jit(solution)/shard_map/ppermute | solution.py:118
  587.5 37.7 %collective-permute-start.13 = (bf16[128,6144]{1,0:T(8,128)(2,1)S(1)}, bf16[128,6144]{1,0:T(8,128)(2,1)S(1)}, u32[]{:S(2)}, u32[]{:S(2)}) collective-permute-start(bf16[128,6144]{1,0:T(8,128)(2,1)S(1)} %collective-permute-done.12), channel_id=1, source_target_pairs={{0,16},{1,17},{2,18},{3,19},{4,20},{5,21},{6,22},{7,23},{8,24},{9,... | collective-permute-start | bytes 4718600 | tf_op jit(solution)/shard_map/ppermute | solution.py:84
  594.9 34.5 %collective-permute-start.65 = (bf16[32,6144]{1,0:T(8,128)(2,1)}, bf16[32,6144]{1,0:T(8,128)(2,1)S(1)}, u32[]{:S(2)}, u32[]{:S(2)}) collective-permute-start(bf16[32,6144]{1,0:T(8,128)(2,1)} %get-tuple-element.34), channel_id=1, source_target_pairs={{16,0},{0,4},{4,8},{8,12},{17,1},{1,5},{5,9},{9,13},{18,2},{2,6},{... | collective-permute-start | bytes 1179656 | tf_op jit(solution)/shard_map/ppermute | solution.py:162
  629.5 17.0 %collective-permute-start.78 = (f16[32,6144]{1,0:T(8,128)(2,1)}, f16[32,6144]{1,0:T(8,128)(2,1)S(1)}, u32[]{:S(2)}, u32[]{:S(2)}) collective-permute-start(f16[32,6144]{1,0:T(8,128)(2,1)} %fusion.237), channel_id=1, source_target_pairs={{20,16},{21,17},{22,18},{23,19}} | collective-permute-start | bytes 1179656 | tf_op jit(solution)/shard_map/ppermute | solution.py:148
  640.0 17.7 %collective-permute-start.83 = (bf16[32,6144]{1,0:T(8,128)(2,1)S(1)}, bf16[32,6144]{1,0:T(8,128)(2,1)S(1)}, u32[]{:S(2)}, u32[]{:S(2)}) collective-permute-start(bf16[32,6144]{1,0:T(8,128)(2,1)S(1)} %copy-done.10), channel_id=1, source_target_pairs={{28,12},{12,8},{8,4},{4,0},{29,13},{13,9},{9,5},{5,1},{30,14},{14,... | collective-permute-start | bytes 1179656 | tf_op jit(solution)/shard_map/ppermute | solution.py:162
  641.3 25.4 %collective-permute-start.73 = (bf16[32,6144]{1,0:T(8,128)(2,1)S(1)}, bf16[32,6144]{1,0:T(8,128)(2,1)S(1)}, u32[]{:S(2)}, u32[]{:S(2)}) collective-permute-start(bf16[32,6144]{1,0:T(8,128)(2,1)S(1)} %get-tuple-element.30), channel_id=1, source_target_pairs={{16,0},{0,4},{4,8},{8,12},{17,1},{1,5},{5,9},{9,13},{18,2},{2,6},{... | collective-permute-start | bytes 1179656 | tf_op jit(solution)/shard_map/ppermute | solution.py:162
  646.5 26.6 %collective-permute-start.71 = (bf16[32,6144]{1,0:T(8,128)(2,1)S(1)}, bf16[32,6144]{1,0:T(8,128)(2,1)S(1)}, u32[]{:S(2)}, u32[]{:S(2)}) collective-permute-start(bf16[32,6144]{1,0:T(8,128)(2,1)S(1)} %get-tuple-element.31), channel_id=1, source_target_pairs={{16,0},{0,4},{4,8},{8,12},{17,1},{1,5},{5,9},{9,13},{18,2},{2,6},{... | collective-permute-start | bytes 1179656 | tf_op jit(solution)/shard_map/ppermute | solution.py:162
  651.8 61.7 %collective-permute-start.53 = (bf16[128,6144]{1,0:T(8,128)(2,1)S(1)}, bf16[128,6144]{1,0:T(8,128)(2,1)S(1)}, u32[]{:S(2)}, u32[]{:S(2)}) collective-permute-start(bf16[128,6144]{1,0:T(8,128)(2,1)S(1)} %collective-permute-done.52), channel_id=1, source_target_pairs={{0,16},{1,17},{2,18},{3,19},{4,20},{5,21},{6,22},{7,23},{8,24},{9,... | collective-permute-start | bytes 4718600 | tf_op jit(solution)/shard_map/ppermute | solution.py:84
  657.7 24.4 %collective-permute-start.89 = (bf16[32,6144]{1,0:T(8,128)(2,1)S(1)}, bf16[32,6144]{1,0:T(8,128)(2,1)S(1)}, u32[]{:S(2)}, u32[]{:S(2)}) collective-permute-start(bf16[32,6144]{1,0:T(8,128)(2,1)S(1)} %collective-permute-done.85), channel_id=1, source_target_pairs={{12,8},{8,4},{4,0},{13,9},{9,5},{5,1},{14,10},{10,6},{6,2},{15,11}... | collective-permute-start | bytes 1179656 | tf_op jit(solution)/shard_map/ppermute | solution.py:162
  666.7 20.8 %collective-permute-start.88 = (bf16[32,6144]{1,0:T(8,128)(2,1)S(1)}, bf16[32,6144]{1,0:T(8,128)(2,1)S(1)}, u32[]{:S(2)}, u32[]{:S(2)}) collective-permute-start(bf16[32,6144]{1,0:T(8,128)(2,1)S(1)} %collective-permute-done.83), channel_id=1, source_target_pairs={{12,8},{8,4},{4,0},{13,9},{9,5},{5,1},{14,10},{10,6},{6,2},{15,11}... | collective-permute-start | bytes 1179656 | tf_op jit(solution)/shard_map/ppermute | solution.py:162
  678.6 17.2 %collective-permute-start.79 = (bf16[32,6144]{1,0:T(8,128)(2,1)S(1)}, bf16[32,6144]{1,0:T(8,128)(2,1)S(1)}, u32[]{:S(2)}, u32[]{:S(2)}) collective-permute-start(bf16[32,6144]{1,0:T(8,128)(2,1)S(1)} %get-tuple-element.27), channel_id=1, source_target_pairs={{16,0},{0,4},{4,8},{8,12},{17,1},{1,5},{5,9},{9,13},{18,2},{2,6},{... | collective-permute-start | bytes 1179656 | tf_op jit(solution)/shard_map/ppermute | solution.py:162
  682.1 20.4 %collective-permute-start.93 = (bf16[32,6144]{1,0:T(8,128)(2,1)S(1)}, bf16[32,6144]{1,0:T(8,128)(2,1)S(1)}, u32[]{:S(2)}, u32[]{:S(2)}) collective-permute-start(bf16[32,6144]{1,0:T(8,128)(2,1)S(1)} %collective-permute-done.89), channel_id=1, source_target_pairs={{8,4},{4,0},{9,5},{5,1},{10,6},{6,2},{11,7},{7,3}} | collective-permute-start | bytes 1179656 | tf_op jit(solution)/shard_map/ppermute | solution.py:162
  687.5 18.2 %collective-permute-start.92 = (bf16[32,6144]{1,0:T(8,128)(2,1)S(1)}, bf16[32,6144]{1,0:T(8,128)(2,1)S(1)}, u32[]{:S(2)}, u32[]{:S(2)}) collective-permute-start(bf16[32,6144]{1,0:T(8,128)(2,1)S(1)} %collective-permute-done.88), channel_id=1, source_target_pairs={{8,4},{4,0},{9,5},{5,1},{10,6},{6,2},{11,7},{7,3}} | collective-permute-start | bytes 1179656 | tf_op jit(solution)/shard_map/ppermute | solution.py:162
  688.8 18.2 %collective-permute-start.87 = (bf16[32,6144]{1,0:T(8,128)(2,1)S(1)}, bf16[32,6144]{1,0:T(8,128)(2,1)S(1)}, u32[]{:S(2)}, u32[]{:S(2)}) collective-permute-start(bf16[32,6144]{1,0:T(8,128)(2,1)S(1)} %collective-permute-done.81), channel_id=1, source_target_pairs={{0,4},{4,8},{8,12},{1,5},{5,9},{9,13},{2,6},{6,10},{10,14},{3,7},{... | collective-permute-start | bytes 1179656 | tf_op jit(solution)/shard_map/ppermute | solution.py:162
  695.9 16.7 %collective-permute-start.86 = (bf16[32,6144]{1,0:T(8,128)(2,1)S(1)}, bf16[32,6144]{1,0:T(8,128)(2,1)S(1)}, u32[]{:S(2)}, u32[]{:S(2)}) collective-permute-start(bf16[32,6144]{1,0:T(8,128)(2,1)S(1)} %collective-permute-done.79), channel_id=1, source_target_pairs={{0,4},{4,8},{8,12},{1,5},{5,9},{9,13},{2,6},{6,10},{10,14},{3,7},{... | collective-permute-start | bytes 1179656 | tf_op jit(solution)/shard_map/ppermute | solution.py:162
  702.5 37.1 %collective-permute-start.55 = (bf16[128,6144]{1,0:T(8,128)(2,1)S(1)}, bf16[128,6144]{1,0:T(8,128)(2,1)S(1)}, u32[]{:S(2)}, u32[]{:S(2)}) collective-permute-start(bf16[128,6144]{1,0:T(8,128)(2,1)S(1)} %collective-permute-done.54), channel_id=1, source_target_pairs={{0,16},{1,17},{2,18},{3,19},{4,20},{5,21},{6,22},{7,23},{8,24},{9,... | collective-permute-start | bytes 4718600 | tf_op jit(solution)/shard_map/ppermute | solution.py:84
  705.8 36.5 %collective-permute-start.97 = (bf16[32,6144]{1,0:T(8,128)(2,1)S(1)}, bf16[32,6144]{1,0:T(8,128)(2,1)S(1)}, u32[]{:S(2)}, u32[]{:S(2)}) collective-permute-start(bf16[32,6144]{1,0:T(8,128)(2,1)S(1)} %collective-permute-done.93), channel_id=1, source_target_pairs={{4,0},{5,1},{6,2},{7,3}} | collective-permute-start | bytes 1179656 | tf_op jit(solution)/shard_map/ppermute | solution.py:162
  707.1 35.2 %collective-permute-start.96 = (bf16[32,6144]{1,0:T(8,128)(2,1)S(1)}, bf16[32,6144]{1,0:T(8,128)(2,1)S(1)}, u32[]{:S(2)}, u32[]{:S(2)}) collective-permute-start(bf16[32,6144]{1,0:T(8,128)(2,1)S(1)} %collective-permute-done.92), channel_id=1, source_target_pairs={{4,0},{5,1},{6,2},{7,3}} | collective-permute-start | bytes 1179656 | tf_op jit(solution)/shard_map/ppermute | solution.py:162
  712.6 27.2 %collective-permute-start.91 = (bf16[32,6144]{1,0:T(8,128)(2,1)S(1)}, bf16[32,6144]{1,0:T(8,128)(2,1)S(1)}, u32[]{:S(2)}, u32[]{:S(2)}) collective-permute-start(bf16[32,6144]{1,0:T(8,128)(2,1)S(1)} %collective-permute-done.87), channel_id=1, source_target_pairs={{4,8},{8,12},{5,9},{9,13},{6,10},{10,14},{7,11},{11,15}} | collective-permute-start | bytes 1179656 | tf_op jit(solution)/shard_map/ppermute | solution.py:162
  713.5 27.0 %collective-permute-start.90 = (bf16[32,6144]{1,0:T(8,128)(2,1)S(1)}, bf16[32,6144]{1,0:T(8,128)(2,1)S(1)}, u32[]{:S(2)}, u32[]{:S(2)}) collective-permute-start(bf16[32,6144]{1,0:T(8,128)(2,1)S(1)} %collective-permute-done.86), channel_id=1, source_target_pairs={{4,8},{8,12},{5,9},{9,13},{6,10},{10,14},{7,11},{11,15}} | collective-permute-start | bytes 1179656 | tf_op jit(solution)/shard_map/ppermute | solution.py:162
  778.6 95.9 %collective-permute-start.98 = (bf16[2,128,1536]{2,1,0:T(8,128)(2,1)}, bf16[2,128,1536]{2,1,0:T(8,128)(2,1)}, u32[]{:S(2)}, u32[]{:S(2)}) collective-permute-start(bf16[2,128,1536]{2,1,0:T(8,128)(2,1)} %get-tuple-element.78), channel_id=1, source_target_pairs={{0,1},{1,2},{2,3},{3,0},{4,5},{5,6},{6,7},{7,4},{8,9},{9,10},{10,1... | collective-permute-start | bytes 2359304 | tf_op jit(solution)/shard_map/ppermute | solution.py:184
  802.6 71.9 %collective-permute-start.99 = (bf16[2,128,1536]{2,1,0:T(8,128)(2,1)}, bf16[2,128,1536]{2,1,0:T(8,128)(2,1)}, u32[]{:S(2)}, u32[]{:S(2)}) collective-permute-start(bf16[2,128,1536]{2,1,0:T(8,128)(2,1)} %get-tuple-element.79), channel_id=1, source_target_pairs={{0,2},{1,3},{2,0},{3,1},{4,6},{5,7},{6,4},{7,5},{8,10},{9,11},{10,... | collective-permute-start | bytes 2359304 | tf_op jit(solution)/shard_map/ppermute | solution.py:184
  809.8 64.7 %collective-permute-start.100 = (bf16[2,128,1536]{2,1,0:T(8,128)(2,1)}, bf16[2,128,1536]{2,1,0:T(8,128)(2,1)}, u32[]{:S(2)}, u32[]{:S(2)}) collective-permute-start(bf16[2,128,1536]{2,1,0:T(8,128)(2,1)} %get-tuple-element.80), channel_id=1, source_target_pairs={{0,3},{1,0},{2,1},{3,2},{4,7},{5,4},{6,5},{7,6},{8,11},{9,8},{10,9... | collective-permute-start | bytes 2359304 | tf_op jit(solution)/shard_map/ppermute | solution.py:184
  876.8 32.4 %collective-permute-start.101 = (f32[128,1536]{1,0:T(8,128)S(1)}, f32[128,1536]{1,0:T(8,128)S(1)}, u32[]{:S(2)}, u32[]{:S(2)}) collective-permute-start(f32[128,1536]{1,0:T(8,128)S(1)} %slice_bitcast_fusion), channel_id=1, source_target_pairs={{0,16},{1,17},{2,18},{3,19},{4,20},{5,21},{6,22},{7,23},{8,24},{9,... | collective-permute-start | bytes 2359304 | tf_op jit(solution)/shard_map/ppermute | solution.py:188
  (65 other events, 1690.9 us)
Sparse Core Ops, SparseCore 0:
  56.9 30.6 all-gather.1
